TPU v7x, 32 devices: a whole 2x2x4 slice. The times are simulated.
32 devices in a mesh: px: 8 (over y, x, core), py: 4 (over z).
Axes of the slice: x: 2, y: 2, z: 4, core: 2. Of those that a mesh axis runs over, the one named last changes fastest.
Arguments:
- displacement: float32 [60, 16, 8, 128], P(None, 'px', 'py'), may hold values from -4 to 4
- velocity: float32 [60, 16, 8, 128], P(None, 'px', 'py'), may hold values from -6 to 6
- modulus: float32 [16, 8, 128], P('px', 'py'), may hold values from 0.5 to 4
- gradient_map: float32 [243, 60], replicated, may hold values from -0.75 to 0.75
- trace_map: float32 [6, 54, 60], replicated, may hold values from -0.75 to 0.75
- lift_map: float32 [6, 60, 54], replicated, may hold values from -0.3125 to 0.3125
- split_map: float32 [27, 27], replicated, may hold values from -1.25 to 1.25
- spread_map: float32 [6, 60, 27], replicated, may hold values from -1.25 to 1.25
- fracture_faces: int32 [32, 512], P(('px', 'py')), may hold values from 0 to 1534, as said below
- fracture_counts: int32 [32, 3], P(('px', 'py')), may hold values from 0 to 256, as said below
Outputs:
- displacement_out: float32 [60, 16, 8, 128], P(None, 'px', 'py')
- velocity_out: float32 [60, 16, 8, 128], P(None, 'px', 'py')
Inputs may be any that keep to these rules, and one draw needn't show every extreme that they name: `fracture_faces`: row p holds the device at index p of px+py (px major). With local element numbers (i * 2 + j) * 128 + k and face ids d * 2 * 2 * 128 + element, slots 0 to 127 name +x faces of elements with i = 1, the next 128 slots +y faces of elements with j = 1, the last 256 slots faces whose neighbour lies on the same device. All ids of a row differ. Only the first fracture_counts[p, s] slots of section s open. `fracture_counts`: counts of opened slots in the three sections of a row. The first is 0 on devices with the last px index, the second on devices with the last py index; over all devices the sections reach 128, 128 and 256.
All inputs are finite; a program needn't handle non-finite values.
Results may differ from a plain program's by a relative error of at most 0.0003.
Values sent between devices are 32-bit elements; how exact they have to be, the bound alone decides.
A program may use at most 64 MiB of HBM per device.

v0:
```python
import functools

import jax
import jax.numpy as jnp
from jax import lax
from jax.experimental import pallas as pl
from jax.experimental.pallas import tpu as pltpu
from jax.sharding import PartitionSpec as P

BLK_CAP = 128
penalty = 2.0
damping = 0.5
substep = 0.1
F32 = jnp.float32
BF16 = jnp.bfloat16
MESH = pl.DeviceIdType.MESH


def halves(value):
    high = value.astype(BF16)
    return high, (value - high.astype(F32)).astype(BF16)


def mm(a, b):
    return jnp.dot(a, b, preferred_element_type=F32)


def kernel(
    disp, vel, mod, grad, trace, lift, split, spread, faces, counts,
    out_u, out_w,
    state, state_b, wa_h, wa_l, lb_h, lb_hl, ew_hl, tp, gp, lp, pp, qp, proj,
    early_h, early_l, late_h, late_l, jump_h, jump_l, send, recv, send_sem, recv_sem,
):
    px, py = lax.axis_index("px"), lax.axis_index("py")
    nx, ny = lax.axis_size("px"), lax.axis_size("py")
    there = (px > 0, px < nx - 1, py > 0, py < ny - 1)
    beside = ({"px": px - 1}, {"px": px + 1}, {"py": py - 1}, {"py": py + 1})
    barrier = pltpu.get_barrier_semaphore()
    for side in range(4):

        @pl.when(there[side])
        def _(side=side):
            pl.semaphore_signal(barrier, inc=1, device_id=beside[side], device_id_type=MESH)

    state[...] = jnp.zeros_like(state)
    for k in range(4):
        lanes = slice(128 * k, 128 * k + 128)
        state[0:60, lanes] = disp[pl.ds(k, 60, stride=4), :]
        state[64:124, lanes] = vel[pl.ds(k, 60, stride=4), :]

    tp[...] = jnp.zeros_like(tp)
    lp[...] = jnp.zeros_like(lp)
    pp[...] = jnp.zeros_like(pp)
    qp[...] = jnp.zeros_like(qp)
    gp[...] = jnp.zeros_like(gp)
    gp[0:243, 0:60] = grad[...]
    qp[0:27, 0:27] = split[...]
    for f in range(6):
        tp[f, 0:27, 0:60] = trace[f, 0:27, :]
        tp[f, 32:59, 0:60] = trace[f, 27:54, :]
        lp[f, 0:60, 0:54] = lift[f]
        pp[64 * f : 64 * f + 60, 0:27] = spread[f]

    def put_a(row, value):
        high, low = halves(value)
        rows = slice(row, row + value.shape[0])
        wa_h[rows, 0:128] = high
        wa_h[rows, 128:256] = high
        wa_l[rows, :] = low

    for f in range(6):
        tv, tt = tp[f, 0:32, :], tp[f, 32:64, :]
        rate = pltpu.roll(damping * tv, 64, 1)
        put_a(64 * f, penalty * tv + 0.5 * tt + rate)
        put_a(64 * f + 32, tv)
        put_a(384 + 32 * f, penalty * tv - 0.5 * tt + rate)
    put_a(576, gp[...])

    def put_b(column, value):
        high, low = halves(value)
        columns = slice(column, column + value.shape[1])
        lb_h[:, columns] = high
        lb_hl[0:64, columns] = high
        lb_hl[64:128, columns] = low

    lane = lax.broadcasted_iota(jnp.int32, (64, 128), 1)

    def lift_part(f):
        full = lp[f]
        lower = pltpu.roll(jnp.where(lane >= 27, 0.5 * full, 0.0), 5, 1)
        return jnp.where(lane < 27, full, 0.0) + lower

    for d in range(3):
        put_b(128 * d, lift_part(2 * d) + pltpu.roll(lift_part(2 * d + 1), 64, 1))
    put_b(384, -jnp.transpose(gp[...])[0:64, :])
    opened = jnp.dot(pp[...], qp[...], precision=lax.Precision.HIGHEST, preferred_element_type=F32)
    for half in range(2):
        part = jnp.zeros((64, 128), F32)
        for f in range(4 * half, min(6, 4 * half + 4)):
            turned = opened[64 * f : 64 * f + 64]
            part = part + (pltpu.roll(turned, 32 * (f % 4), 1) if f % 4 else turned)
        high, low = halves(-part)
        ew_hl[0:64, 128 * half : 128 * half + 128] = high
        ew_hl[64:128, 128 * half : 128 * half + 128] = low

    jump_h[192:256, :] = jnp.zeros((64, 512), BF16)
    jump_l[192:256, :] = jnp.zeros((64, 512), BF16)

    ids = faces[...]
    slots = lax.broadcasted_iota(jnp.int32, ids.shape, 1)
    limit = jnp.where(
        slots < BLK_CAP,
        counts[0, 0],
        jnp.where(slots < 2 * BLK_CAP, BLK_CAP + counts[0, 1], 2 * BLK_CAP + counts[0, 2]),
    )
    group = jnp.where(slots < limit, ids >> 7, -1)
    spot = ids & 127
    high_hot = lax.broadcasted_iota(jnp.int32, (16, ids.shape[1]), 0) == group
    low_hot = lax.broadcasted_iota(jnp.int32, (128, ids.shape[1]), 0) == spot
    open_mask = lax.dot_general(
        high_hot.astype(F32).astype(BF16),
        low_hot.astype(F32).astype(BF16),
        (((1,), (1,)), ((), ())),
        preferred_element_type=F32,
    )

    for slot, side in ((0, 1), (1, 0), (2, 3), (3, 2)):

        @pl.when(jnp.logical_not(there[side]))
        def _(slot=slot):
            for s in range(3):
                recv[s, slot] = jnp.zeros((64, 256), F32)

    pl.semaphore_wait(barrier, sum(t.astype(jnp.int32) for t in there))

    alive = [jnp.where(t, 1.0, 0.0).astype(F32) for t in there]
    lane_row = lax.broadcasted_iota(jnp.int32, (1, 128), 1)
    not_first = (lane_row > 0).astype(F32)
    not_last = (lane_row < 127).astype(F32)
    copies = [
        [
            pltpu.make_async_remote_copy(
                src_ref=send.at[s, side],
                dst_ref=recv.at[s, side],
                send_sem=send_sem.at[s, side],
                recv_sem=recv_sem.at[s, side],
                device_id=beside[side],
                device_id_type=MESH,
            )
            for side in range(4)
        ]
        for s in range(3)
    ]
    outer = ((0, 1), (2, 3), (0, 2), (1, 3))

    def block(k):
        return slice(128 * k, 128 * k + 128)

    for s in range(3):
        for k in range(4):
            high, low = halves(state[:, block(k)])
            state_b[0:128, block(k)] = high
            state_b[128:256, block(k)] = low
        proj[0:256, :] = mm(wa_h[0:256, :], state_b[...]) + mm(wa_l[0:256, :], state_b[0:128, :])
        for f in range(4):
            for half in range(2):
                k = outer[f][half]
                send[s, f, :, block(half)] = proj[64 * f : 64 * f + 64, block(k)]
                if s == 2 and f % 2 == 1:
                    row = 4 * (f // 2) + k
                    send[s, f, 27:28, block(half)] = open_mask[row : row + 1, :]
        for side in range(4):

            @pl.when(there[side])
            def _(s=s, side=side):
                copies[s][side].start()

        proj[256:832, :] = mm(wa_h[256:832, :], state_b[...]) + mm(
            wa_l[256:832, :], state_b[0:128, :]
        )

        def own(f):
            return 64 * f, 384 + 32 * f

        def difference(f, k, upper, lower):
            at, at_q = own(f)
            return (
                upper - proj[at_q : at_q + 32, block(k)],
                lower - proj[at + 32 : at + 64, block(k)],
            )

        def put(high_ref, low_ref, row, k, value):
            high, low = halves(value)
            rows = slice(row, row + value.shape[0])
            high_ref[rows, block(k)] = high
            low_ref[rows, block(k)] = low

        for k in range(4):
            for f in (4, 5):
                shift, mask = (1, not_first) if f == 4 else (127, not_last)
                other = 64 * (9 - f)
                upper = pltpu.roll(proj[other : other + 32, block(k)], shift, 1)
                lower = pltpu.roll(proj[other + 32 : other + 64, block(k)], shift, 1)
                upper, lower = difference(f, k, upper, lower)
                put(early_h, early_l, 64 * (f - 4), k, upper * mask)
                put(early_h, early_l, 64 * (f - 4) + 32, k, lower * mask)
                if s == 2:
                    opens = open_mask[8 + k : 9 + k, :]
                    if f == 4:
                        opens = pltpu.roll(opens, 1, 1)
                    put(jump_h, jump_l, 32 * f, k, lower * mask * opens)
            put(early_h, early_l, 128, k, proj[576:832, block(k)] * mod[k : k + 1, :])
        both = mm(lb_hl[:, 256:640], early_h[...])
        force = both[0:64] + both[64:128] + mm(lb_h[:, 256:640], early_l[...])

        for side in range(4):

            @pl.when(there[side])
            def _(s=s, side=side):
                copies[s][side ^ 1].wait_recv()

        for k in range(4):
            i, j = k // 2, k % 2
            for f in range(4):
                inner = (i, 1 - i, j, 1 - j)[f] == 1
                n = k ^ (2 if f < 2 else 1)
                if inner:
                    at = 64 * (f ^ 1)
                    upper, lower = proj[at : at + 32, block(n)], proj[at + 32 : at + 64, block(n)]
                else:
                    half = j if f < 2 else i
                    upper, lower = (
                        recv[s, f ^ 1, 0:32, block(half)],
                        recv[s, f ^ 1, 32:64, block(half)],
                    )
                upper, lower = difference(f, k, upper, lower)
                if not inner:
                    upper, lower = upper * alive[f], lower * alive[f]
                put(late_h, late_l, 64 * f, k, upper)
                put(late_h, late_l, 64 * f + 32, k, lower)
                if s == 2:
                    row = 4 * (f // 2)
                    if f % 2:
                        opens = open_mask[row + k : row + k + 1, :]
                    elif inner:
                        opens = open_mask[row + n : row + n + 1, :]
                    else:
                        opens = recv[s, f ^ 1, 27:28, block(half)]
                    put(jump_h, jump_l, 32 * f, k, lower * opens)
        both = mm(lb_hl[:, 0:256], late_h[...])
        force = force + both[0:64] + both[64:128] + mm(lb_h[:, 0:256], late_l[...])
        velocity = state[64:128, :] + substep * force
        displace = state[0:64, :] + substep * velocity
        if s < 2:
            state[64:128, :] = velocity
            state[0:64, :] = displace
        else:
            both = mm(ew_hl[...], jump_h[...])
            displace = displace + both[0:64] + both[64:128] + mm(ew_hl[0:64, :], jump_l[...])
            for k in range(4):
                out_u[pl.ds(k, 60, stride=4), :] = displace[0:60, block(k)]
                out_w[pl.ds(k, 60, stride=4), :] = velocity[0:60, block(k)]

    for s in range(3):
        for side in range(4):

            @pl.when(there[side])
            def _(s=s, side=side):
                copies[s][side].wait_send()


def shards(
    displacement, velocity, modulus, gradient_map, trace_map, lift_map, split_map, spread_map,
    fracture_faces, fracture_counts,
):
    shape = displacement.shape
    components = shape[0]
    flat = (components * 4, 128)
    vmem = pl.BlockSpec(memory_space=pltpu.VMEM)
    smem = pl.BlockSpec(memory_space=pltpu.SMEM)
    out = jax.ShapeDtypeStruct(flat, F32)
    u, w = pl.pallas_call(
        kernel,
        out_shape=(out, out),
        in_specs=[vmem] * 9 + [smem],
        out_specs=(vmem, vmem),
        scratch_shapes=[
            pltpu.VMEM((128, 512), F32),
            pltpu.VMEM((256, 512), BF16),
            pltpu.VMEM((832, 256), BF16),
            pltpu.VMEM((832, 128), BF16),
            pltpu.VMEM((64, 640), BF16),
            pltpu.VMEM((128, 640), BF16),
            pltpu.VMEM((128, 256), BF16),
            pltpu.VMEM((6, 64, 128), F32),
            pltpu.VMEM((256, 128), F32),
            pltpu.VMEM((6, 64, 128), F32),
            pltpu.VMEM((384, 128), F32),
            pltpu.VMEM((128, 128), F32),
            pltpu.VMEM((832, 512), F32),
            pltpu.VMEM((384, 512), BF16),
            pltpu.VMEM((384, 512), BF16),
            pltpu.VMEM((256, 512), BF16),
            pltpu.VMEM((256, 512), BF16),
            pltpu.VMEM((256, 512), BF16),
            pltpu.VMEM((256, 512), BF16),
            pltpu.VMEM((3, 4, 64, 256), F32),
            pltpu.VMEM((3, 4, 64, 256), F32),
            pltpu.SemaphoreType.DMA((3, 4)),
            pltpu.SemaphoreType.DMA((3, 4)),
        ],
        compiler_params=pltpu.CompilerParams(
            collective_id=0, has_side_effects=True, vmem_limit_bytes=40 * 1024 * 1024
        ),
    )(
        displacement.reshape(flat),
        velocity.reshape(flat),
        modulus.reshape(4, 128),
        gradient_map,
        trace_map,
        lift_map,
        split_map,
        spread_map,
        fracture_faces,
        fracture_counts,
    )
    return u.reshape(shape), w.reshape(shape)


def solution(mesh):
    return jax.shard_map(
        shards,
        mesh=mesh,
        in_specs=(
            P(None, "px", "py", None),
            P(None, "px", "py", None),
            P("px", "py", None),
            P(),
            P(),
            P(),
            P(),
            P(),
            P(("px", "py"), None),
            P(("px", "py"), None),
        ),
        out_specs=(P(None, "px", "py", None), P(None, "px", "py", None)),
        check_vma=False,
    )
```

profile of v0, /device:TPU:0, one launch (start us, length us, event | category | flops | bytes accessed | tf_op | source)
XLA Modules:
  0.0 22.1 jit_solution(14374525071077135672)
XLA Ops:
  0.6 0.0 copy-start.7
  0.6 1.0 %copy.12.grad = f32[243,60]{1,0:T(8,128)S(1)} copy(f32[243,60]{0,1:T(8,128)} %param.13) | data formatting | bytes 116640 | tf_op args[3]
  1.6 0.0 copy-done.7
  1.6 0.0 copy-start.8
  1.6 0.0 copy-start.2
  1.6 0.0 copy-start.3
  1.7 0.0 copy-start.4
  1.7 0.0 copy-start.5
  1.7 0.0 copy-start.6
  1.7 0.1 copy.13.lift
  1.8 0.7 %copy-done.8 = f32[6,60,27]{1,2,0:T(8,128)S(1)} copy-done((f32[6,60,27]{1,2,0:T(8,128)S(1)}, f32[6,60,27]{1,2,0:T(8,128)}, u32[]{:S(2)}) %copy-start.8) | copy-done | bytes 38904
  2.5 0.0 copy-start
  2.5 0.0 copy-start.1
  2.5 0.1 copy.14.spread
  2.7 0.0 copy-done.2
  2.7 0.0 copy-done.3
  2.7 0.0 copy-done.4
  2.7 0.0 copy-done.5
  2.7 0.0 copy-done.6
  2.7 0.7 %copy-done = f32[6,54,60]{2,1,0:T(8,128)S(1)} copy-done((f32[6,54,60]{2,1,0:T(8,128)S(1)}, f32[6,54,60]{2,1,0:T(8,128)}, u32[]{:S(2)}) %copy-start) | copy-done | bytes 77784
  3.5 0.1 copy-done.1
  3.5 17.2 %shard_map.113 = (f32[240,128]{1,0:T(8,128)S(1)}, f32[240,128]{1,0:T(8,128)S(1)}) custom-call(f32[240,128]{1,0:T(8,128)S(1)} %bitcast.5, f32[240,128]{1,0:T(8,128)S(1)} %bitcast.6, f32[4,128]{1,0:T(4,128)S(1)} %bitcast.9, f32[243,60]{1,0:T(8,128)S(1)} %copy.12.grad, f32[6,54,60]{2,1,0:T(8,128)S(1)} %copy-done, f32[6,60,54]{2,1,0:T(8,128)S(1)} %copy.13.lift, ...), custom_call_target="tpu_custom_call" | custom-call | tf_op jit(solution)/shard_map/pallas_call | solution.py:282
  20.8 0.7 %copy.17 = f32[60,2,2,128]{3,2,1,0:T(2,128)} copy(f32[60,2,2,128]{3,2,1,0:T(2,128)S(1)} %bitcast.8) | data formatting | bytes 245760
  21.4 0.6 %copy.18 = f32[60,2,2,128]{3,2,1,0:T(2,128)} copy(f32[60,2,2,128]{3,2,1,0:T(2,128)S(1)} %bitcast.7) | data formatting | bytes 245760
Async XLA Ops:
  0.6 1.0 %copy-start.7 = (f32[6,60,54]{1,2,0:T(8,128)S(1)}, f32[6,60,54]{1,2,0:T(8,128)}, u32[]{:S(2)}) copy-start(f32[6,60,54]{1,2,0:T(8,128)} %param.15) | copy-start | bytes 233284
  1.6 0.9 %copy-start.8 = (f32[6,60,27]{1,2,0:T(8,128)S(1)}, f32[6,60,27]{1,2,0:T(8,128)}, u32[]{:S(2)}) copy-start(f32[6,60,27]{1,2,0:T(8,128)} %param.17) | copy-start | bytes 116644
  1.6 1.0 %copy-start.2 = (f32[60,2,2,128]{3,2,1,0:T(2,128)S(1)}, f32[60,2,2,128]{3,2,1,0:T(2,128)}, u32[]{:S(2)}) copy-start(f32[60,2,2,128]{3,2,1,0:T(2,128)} %param.11) | copy-start | bytes 368644
  1.6 1.0 %copy-start.3 = (f32[27,27]{1,0:T(8,128)S(1)}, f32[27,27]{1,0:T(8,128)}, u32[]{:S(2)}) copy-start(f32[27,27]{1,0:T(8,128)} %split.1) | copy-start | bytes 8752
  1.7 1.0 %copy-start.4 = (f32[2,2,128]{2,1,0:T(2,128)S(1)}, f32[2,2,128]{2,1,0:T(2,128)}, u32[]{:S(2)}) copy-start(f32[2,2,128]{2,1,0:T(2,128)} %param.12) | copy-start | bytes 6148
  1.7 1.0 %copy-start.5 = (s32[1,512]{1,0:T(1,128)S(1)}, s32[1,512]{1,0:T(1,128)}, u32[]{:S(2)}) copy-start(s32[1,512]{1,0:T(1,128)} %faces.1) | copy-start | bytes 6148
  1.7 1.0 %copy-start.6 = (s32[1,3]{1,0:T(1,128)S(1)}, s32[1,3]{1,0:T(1,128)}, u32[]{:S(2)}) copy-start(s32[1,3]{1,0:T(1,128)} %counts.1) | copy-start | bytes 40
  2.5 0.9 %copy-start = (f32[6,54,60]{2,1,0:T(8,128)S(1)}, f32[6,54,60]{2,1,0:T(8,128)}, u32[]{:S(2)}) copy-start(f32[6,54,60]{2,1,0:T(8,128)} %trace.1) | copy-start | bytes 233284
  2.5 1.0 %copy-start.1 = (f32[60,2,2,128]{3,2,1,0:T(2,128)S(1)}, f32[60,2,2,128]{3,2,1,0:T(2,128)}, u32[]{:S(2)}) copy-start(f32[60,2,2,128]{3,2,1,0:T(2,128)} %param.10) | copy-start | bytes 368644
where the time goes:
time: 22.2 us; the launch traced here: 22.1 us
  Pallas kernels  17.2 us (77%)
  local copies, waits for them, and re-layouts  4.09 us (18%)
  between operations  0.74 us (3%)
    pallas_call x1, Pallas kernels, shards(): pl.pallas_call(kernel, out_shape=(out, out), in_specs=[vmem] * 9 + [smem]...  17.2 us
    unnamed x23, local copies, waits for them, and re-layouts  4.09 us

commit v1 on v0

v1 whole, which is shorter than its diff:
```python
import jax
import jax.numpy as jnp
from jax import lax
from jax.experimental import pallas as pl
from jax.experimental.pallas import tpu as pltpu
from jax.sharding import PartitionSpec as P

BLK_CAP = 128
penalty = 2.0
damping = 0.5
substep = 0.1
F32 = jnp.float32
BF16 = jnp.bfloat16
MESH = pl.DeviceIdType.MESH


def halves(value):
    high = value.astype(BF16)
    return high, (value - high.astype(F32)).astype(BF16)


def mm(a, b):
    return jnp.dot(a, b, preferred_element_type=F32)


def kernel(
    disp_in, vel_in, mod_in, grad_in, trace_in, lift_in, split_in, spread_in, faces_in, counts_in,
    out_u, out_w, out_f,
    disp, vel, mod, grad, trace, lift, split, spread, faces, counts,
    state, state_b, wa_h, wa_l, lb_h, lb_hl, ew_hl, tp, gp, lp, pp, qp, proj,
    early_h, early_l, late_h, late_l, jump_h, jump_l, send, recv, in_sem, send_sem, recv_sem,
):
    px, py = lax.axis_index("px"), lax.axis_index("py")
    nx, ny = lax.axis_size("px"), lax.axis_size("py")
    there = (px > 0, px < nx - 1, py > 0, py < ny - 1)
    beside = ({"px": px - 1}, {"px": px + 1}, {"py": py - 1}, {"py": py + 1})
    barrier = pltpu.get_barrier_semaphore()
    for side in (2, 3, 0, 1):

        @pl.when(there[side])
        def _(side=side):
            pl.semaphore_signal(barrier, inc=1, device_id=beside[side], device_id_type=MESH)

    names = ("trace", "disp", "vel", "grad", "lift", "mod", "spread", "split", "faces", "counts")
    given = (trace_in, disp_in, vel_in, grad_in, lift_in, mod_in, spread_in, split_in, faces_in, counts_in)
    local = (trace, disp, vel, grad, lift, mod, spread, split, faces, counts)
    loads = {}
    for n, name in enumerate(names):
        loads[name] = pltpu.make_async_copy(given[n], local[n], in_sem.at[n])
        loads[name].start()

    for ref in (state, tp, lp, pp, qp, gp):
        ref[...] = jnp.zeros_like(ref)
    for ref in (late_h, late_l, jump_h, jump_l):
        for d in range(ref.shape[0] // 128):
            ref[128 * d + 112 : 128 * d + 128, :] = jnp.zeros((16, 512), BF16)
    for ref in (early_h, early_l):
        ref[112:128, :] = jnp.zeros((16, 512), BF16)
    for slot, side in ((0, 1), (1, 0), (2, 3), (3, 2)):

        @pl.when(jnp.logical_not(there[side]))
        def _(slot=slot):
            for s in range(3):
                recv[s, slot] = jnp.zeros((56, 256), F32)

    def put_a(row, value):
        high, low = halves(value)
        rows = slice(row, row + value.shape[0])
        wa_h[rows, 0:128] = high
        wa_h[rows, 128:256] = high
        wa_l[rows, :] = low

    row_id = lax.broadcasted_iota(jnp.int32, (56, 128), 0)

    def face_rows(f, sign):
        both = tp[f]
        upper = penalty * both + (sign * 0.5) * pltpu.roll(both, 29, 0)
        upper = upper + pltpu.roll(damping * both, 64, 1)
        lower = jnp.where(row_id < 54, pltpu.roll(both, 27, 0), 0.0)
        return jnp.where(row_id < 27, upper, lower)

    def put_faces(row, d, sign):
        pair = [face_rows(2 * d, sign), face_rows(2 * d + 1, sign)]
        put_a(row + 112 * d, jnp.concatenate(pair, axis=0))

    loads["trace"].wait()
    for f in range(6):
        tp[f, 0:54, 0:60] = trace[f]
    put_faces(0, 0, 1.0)
    put_faces(0, 1, 1.0)

    def block(k):
        return slice(128 * k, 128 * k + 128)

    loads["disp"].wait()
    loads["vel"].wait()
    for k in range(4):
        state[0:60, block(k)] = disp[pl.ds(k, 60, stride=4), :]
        state[64:124, block(k)] = vel[pl.ds(k, 60, stride=4), :]

    copies = [
        [
            pltpu.make_async_remote_copy(
                src_ref=send.at[s, side],
                dst_ref=recv.at[s, side],
                send_sem=send_sem.at[s, side],
                recv_sem=recv_sem.at[s, side],
                device_id=beside[side],
                device_id_type=MESH,
            )
            for side in range(4)
        ]
        for s in range(3)
    ]
    outer = ((0, 1), (2, 3), (0, 2), (1, 3))

    def project_outer(s, open_mask=None):
        for k in range(4):
            high, low = halves(state[:, block(k)])
            state_b[0:128, block(k)] = high
            state_b[128:256, block(k)] = low
        for d in (1, 0):
            rows = slice(112 * d, 112 * d + 112)
            proj[rows, :] = mm(wa_h[rows, :], state_b[...]) + mm(wa_l[rows, :], state_b[0:128, :])
            for f in (2 * d, 2 * d + 1):
                for half in range(2):
                    k = outer[f][half]
                    send[s, f, :, block(half)] = proj[56 * f : 56 * f + 56, block(k)]
                    if s == 2 and f % 2 == 1:
                        row = 4 * d + k
                        send[s, f, 54:55, block(half)] = open_mask[row : row + 1, :]
            if s == 0 and d == 1:
                pl.semaphore_wait(barrier, sum(t.astype(jnp.int32) for t in there))
            for side in (2 * d, 2 * d + 1):

                @pl.when(there[side])
                def _(side=side):
                    copies[s][side].start()

    project_outer(0)

    put_faces(0, 2, 1.0)
    for d in range(3):
        put_faces(336, d, -1.0)
    loads["grad"].wait()
    gp[0:60, 0:243] = grad[...]
    put_a(672, jnp.transpose(gp[...]))

    def put_b(column, value):
        high, low = halves(value)
        columns = slice(column, column + value.shape[1])
        lb_h[:, columns] = high
        lb_hl[0:64, columns] = high
        lb_hl[64:128, columns] = low

    put_b(384, -gp[0:64, :])
    loads["lift"].wait()
    lift_row = lax.broadcasted_iota(jnp.int32, (54, 60), 0)
    for f in range(6):
        at = 56 * (f % 2)
        lp[f // 2, at : at + 54, 0:60] = jnp.where(lift_row < 27, lift[f], 0.5 * lift[f])
    for d in range(3):
        put_b(128 * d, jnp.transpose(lp[d])[0:64, :])

    loads["spread"].wait()
    loads["split"].wait()
    qp[0:27, 0:27] = split[...]
    qp[32:59, 0:27] = split[...]
    row128 = lax.broadcasted_iota(jnp.int32, (128, 128), 0)
    placed = jnp.where(row128 < 32, pltpu.roll(qp[...], 27, 1), pltpu.roll(qp[...], 83, 1))
    for f in range(6):
        at = 32 * (f % 2)
        pp[f // 2, at : at + 27, 0:60] = spread[f]
    for d in range(3):
        part = jnp.dot(
            jnp.transpose(pp[d])[0:64, :],
            placed,
            precision=lax.Precision.HIGHEST,
            preferred_element_type=F32,
        )
        high, low = halves(-part)
        ew_hl[0:64, block(d)] = high
        ew_hl[64:128, block(d)] = low

    loads["faces"].wait()
    loads["counts"].wait()
    loads["mod"].wait()
    ids = faces[...]
    slots = lax.broadcasted_iota(jnp.int32, ids.shape, 1)
    section = jnp.where(slots < BLK_CAP, 0, jnp.where(slots < 2 * BLK_CAP, 1, 2))
    limit = jnp.where(
        section == 0,
        counts[0:1, 0:1],
        jnp.where(section == 1, BLK_CAP + counts[0:1, 1:2], 2 * BLK_CAP + counts[0:1, 2:3]),
    )
    group = jnp.where(slots < limit, ids >> 7, -1)
    spot = ids & 127
    high_hot = lax.broadcasted_iota(jnp.int32, (16, ids.shape[1]), 0) == group
    low_hot = lax.broadcasted_iota(jnp.int32, (128, ids.shape[1]), 0) == spot
    open_mask = lax.dot_general(
        high_hot.astype(F32).astype(BF16),
        low_hot.astype(F32).astype(BF16),
        (((1,), (1,)), ((), ())),
        preferred_element_type=F32,
    )

    alive = [jnp.where(t, 1.0, 0.0).astype(F32) for t in there]
    lane_row = lax.broadcasted_iota(jnp.int32, (1, 128), 1)
    not_first = (lane_row > 0).astype(F32)
    not_last = (lane_row < 127).astype(F32)

    def put(high_ref, low_ref, row, k, value):
        high, low = halves(value)
        rows = slice(row, row + value.shape[0])
        high_ref[rows, block(k)] = high
        low_ref[rows, block(k)] = low

    def traced(f, k):
        return proj[56 * f : 56 * f + 56, block(k)]

    def own(f, k):
        return proj[336 + 56 * f : 392 + 56 * f, block(k)]

    for s in range(3):
        if s > 0:
            project_outer(s, open_mask)
        proj[224:928, :] = mm(wa_h[224:928, :], state_b[...]) + mm(
            wa_l[224:928, :], state_b[0:128, :]
        )
        for k in range(4):
            before = (pltpu.roll(traced(5, k), 1, 1) - own(4, k)) * not_first
            after = (pltpu.roll(traced(4, k), 127, 1) - own(5, k)) * not_last
            put(early_h, early_l, 0, k, jnp.concatenate([before, after], axis=0))
            if s == 2:
                opens = open_mask[8 + k : 9 + k, :]
                pair = [before * pltpu.roll(opens, 1, 1), after * opens]
                put(jump_h, jump_l, 256, k, jnp.concatenate(pair, axis=0))
            put(early_h, early_l, 128, k, proj[672:928, block(k)] * mod[k : k + 1, :])
        both = mm(lb_hl[:, 256:640], early_h[...])
        force = both[0:64] + both[64:128] + mm(lb_h[:, 256:640], early_l[...])

        for d in (0, 1):
            for side in (2 * d, 2 * d + 1):

                @pl.when(there[side])
                def _(s=s, side=side):
                    copies[s][side ^ 1].wait_recv()

            for k in range(4):
                i, j = k // 2, k % 2
                n = k ^ (2 if d == 0 else 1)
                half = j if d == 0 else i
                flux, jump = [], []
                for f in (2 * d, 2 * d + 1):
                    inner = (i, 1 - i, j, 1 - j)[f] == 1
                    if inner:
                        part = traced(f ^ 1, n) - own(f, k)
                    else:
                        part = (recv[s, f ^ 1, :, block(half)] - own(f, k)) * alive[f]
                    flux.append(part)
                    if s == 2:
                        if f % 2:
                            opens = open_mask[4 * d + k : 4 * d + k + 1, :]
                        elif inner:
                            opens = open_mask[4 * d + n : 4 * d + n + 1, :]
                        else:
                            opens = recv[s, f ^ 1, 54:55, block(half)]
                        jump.append(part * opens)
                put(late_h, late_l, 128 * d, k, jnp.concatenate(flux, axis=0))
                if s == 2:
                    put(jump_h, jump_l, 128 * d, k, jnp.concatenate(jump, axis=0))
        both = mm(lb_hl[:, 0:256], late_h[...])
        force = force + both[0:64] + both[64:128] + mm(lb_h[:, 0:256], late_l[...])
        if s < 2:
            velocity = state[64:128, :] + substep * force
            state[64:128, :] = velocity
            state[0:64, :] = state[0:64, :] + substep * velocity
        else:
            both = mm(ew_hl[...], jump_h[...])
            displace = state[0:64, :] + both[0:64] + both[64:128] + mm(ew_hl[0:64, :], jump_l[...])
            for k in range(4):
                out_u[pl.ds(k, 60, stride=4), :] = displace[0:60, block(k)]
                out_w[pl.ds(k, 60, stride=4), :] = state[64:124, block(k)]
                out_f[pl.ds(k, 60, stride=4), :] = force[0:60, block(k)]

    for s in range(3):
        for side in range(4):

            @pl.when(there[side])
            def _(s=s, side=side):
                copies[s][side].wait_send()


def shards(
    displacement, velocity, modulus, gradient_map, trace_map, lift_map, split_map, spread_map,
    fracture_faces, fracture_counts,
):
    shape = displacement.shape
    flat = (shape[0] * 4, 128)
    args = (
        displacement.reshape(flat),
        velocity.reshape(flat),
        modulus.reshape(4, 128),
        gradient_map.T,
        trace_map,
        jnp.transpose(lift_map, (0, 2, 1)),
        split_map,
        jnp.transpose(spread_map, (0, 2, 1)),
        fracture_faces,
        fracture_counts,
    )
    vmem = pl.BlockSpec(memory_space=pltpu.VMEM)
    hbm = pl.BlockSpec(memory_space=pltpu.HBM)
    out = jax.ShapeDtypeStruct(flat, F32)
    opened, velocity_now, force = pl.pallas_call(
        kernel,
        out_shape=(out, out, out),
        in_specs=[hbm] * 10,
        out_specs=(vmem, vmem, vmem),
        scratch_shapes=[
            *(pltpu.VMEM(a.shape, a.dtype) for a in args),
            pltpu.VMEM((128, 512), F32),
            pltpu.VMEM((256, 512), BF16),
            pltpu.VMEM((928, 256), BF16),
            pltpu.VMEM((928, 128), BF16),
            pltpu.VMEM((64, 640), BF16),
            pltpu.VMEM((128, 640), BF16),
            pltpu.VMEM((128, 384), BF16),
            pltpu.VMEM((6, 56, 128), F32),
            pltpu.VMEM((128, 256), F32),
            pltpu.VMEM((3, 128, 128), F32),
            pltpu.VMEM((3, 128, 128), F32),
            pltpu.VMEM((128, 128), F32),
            pltpu.VMEM((928, 512), F32),
            pltpu.VMEM((384, 512), BF16),
            pltpu.VMEM((384, 512), BF16),
            pltpu.VMEM((256, 512), BF16),
            pltpu.VMEM((256, 512), BF16),
            pltpu.VMEM((384, 512), BF16),
            pltpu.VMEM((384, 512), BF16),
            pltpu.VMEM((3, 4, 56, 256), F32),
            pltpu.VMEM((3, 4, 56, 256), F32),
            pltpu.SemaphoreType.DMA((10,)),
            pltpu.SemaphoreType.DMA((3, 4)),
            pltpu.SemaphoreType.DMA((3, 4)),
        ],
        compiler_params=pltpu.CompilerParams(
            collective_id=0, has_side_effects=True, vmem_limit_bytes=64 * 1024 * 1024 - 262144
        ),
    )(*args)
    velocity_out = velocity_now + substep * force
    displacement_out = opened + substep * velocity_out
    return displacement_out.reshape(shape), velocity_out.reshape(shape)


def solution(mesh):
    return jax.shard_map(
        shards,
        mesh=mesh,
        in_specs=(
            P(None, "px", "py", None),
            P(None, "px", "py", None),
            P("px", "py", None),
            P(),
            P(),
            P(),
            P(),
            P(),
            P(("px", "py"), None),
            P(("px", "py"), None),
        ),
        out_specs=(P(None, "px", "py", None), P(None, "px", "py", None)),
        check_vma=False,
    )
```

time: 22.2 us -> 19.4 us (0.87)
  local copies, waits for them, and re-layouts: 4.09 us -> 0 us
  other arithmetic: 0 us -> 1.74 us
  Pallas kernels: 17.2 us -> 16.9 us
    unnamed x23 -> x0, local copies, waits for them, and re-layouts: 4.09 us -> none
    add x0 -> x1, other arithmetic: none -> 1.74 us  [shards(): displacement_out = opened + substep * velocity_out]
    pallas_call x1, Pallas kernels: 17.2 us -> 16.9 us  [shards(): pl.pallas_call(kernel, out_shape=(out, out, out), in_specs=[hbm] * 10, ou...]
where the time goes in v1:
time: 19.4 us; the launch traced here: 19.2 us
  Pallas kernels  16.9 us (87%)
  other arithmetic  1.74 us (9%)
  between operations  0.64 us (3%)
    pallas_call x1, Pallas kernels, shards(): pl.pallas_call(kernel, out_shape=(out, out, out), in_specs=[hbm] * 10, ou...  16.9 us
    add x1, other arithmetic, shards(): displacement_out = opened + substep * velocity_out  1.74 us

profile of v1, /device:TPU:0, one launch (start us, length us, event | category | flops | bytes accessed | tf_op | source)
XLA Modules:
  0.0 19.2 jit_solution(9137325413111299360)
XLA Ops:
  0.6 16.9 %shard_map.113 = (f32[240,128]{1,0:T(8,128)}, f32[240,128]{1,0:T(8,128)}, f32[240,128]{1,0:T(8,128)}) custom-call(f32[240,128]{1,0:T(8,128)} %bitcast.11, f32[240,128]{1,0:T(8,128)} %bitcast.12, f32[4,128]{1,0:T(4,128)} %bitcast.15, f32[60,243]{1,0:T(8,128)} %bitcast.14, f32[6,54,60]{2,1,0:T(8,128)} %trace_in.1, f32[6,54,60]{2,1,0:T(8,128)} %bitcast.8, ...), custom_call_target="tpu_custom_call" | custom-call | tf_op jit(solution)/shard_map/pallas_call | solution.py:315
  17.5 1.7 %multiply_add_fusion = (f32[240,128]{1,0:T(8,128)}, f32[240,128]{1,0:T(8,128)}) fusion(f32[240,128]{1,0:T(8,128)} %get-tuple-element.5, f32[240,128]{1,0:T(8,128)} %get-tuple-element.6, f32[240,128]{1,0:T(8,128)} %get-tuple-element.7), kind=kLoop, calls=%fused_computation | loop fusion | flops 122880 | bytes 614400 | tf_op jit(solution)/shard_map/add | solution.py:352

commit v2 on v1

--- a/solution.py
+++ b/solution.py
@@ -345,9 +345,9 @@
             pltpu.SemaphoreType.DMA((3, 4)),
         ],
         compiler_params=pltpu.CompilerParams(
-            collective_id=0, has_side_effects=True, vmem_limit_bytes=64 * 1024 * 1024 - 262144
+            collective_id=0, has_side_effects=True, vmem_limit_bytes=40 * 1024 * 1024
         ),
-    )(*args)
+    )(*(pltpu.with_memory_space_constraint(a, pltpu.HBM) for a in args))
     velocity_out = velocity_now + substep * force
     displacement_out = opened + substep * velocity_out
     return displacement_out.reshape(shape), velocity_out.reshape(shape)

time: 19.4 us -> 17.7 us (0.912)
  other arithmetic: 1.74 us -> 0.72 us
  Pallas kernels: 16.9 us -> 16.1 us
    add x1, other arithmetic: 1.74 us -> 0.72 us  [shards(): displacement_out = opened + substep * velocity_out]
    pallas_call x1, Pallas kernels: 16.9 us -> 16.1 us  [shards(): pl.pallas_call(kernel, out_shape=(out, out, out), in_specs=[hbm] * 10, ou...]
where the time goes in v2:
time: 17.7 us; the launch traced here: 17.5 us
  Pallas kernels  16.1 us (91%)
  other arithmetic  0.72 us (4%)
  between operations  0.64 us (4%)
    pallas_call x1, Pallas kernels, shards(): pl.pallas_call(kernel, out_shape=(out, out, out), in_specs=[hbm] * 10, ou...  16.1 us
    add x1, other arithmetic, shards(): displacement_out = opened + substep * velocity_out  0.72 us

profile of v2, /device:TPU:0, one launch (start us, length us, event | category | flops | bytes accessed | tf_op | source)
XLA Modules:
  0.0 17.5 jit_solution(7192000401398892591)
XLA Ops:
  0.6 16.1 %shard_map.113 = (f32[240,128]{1,0:T(8,128)S(1)}, f32[240,128]{1,0:T(8,128)S(1)}, f32[240,128]{1,0:T(8,128)S(1)}) custom-call(f32[240,128]{1,0:T(8,128)} %bitcast.11, f32[240,128]{1,0:T(8,128)} %bitcast.12, f32[4,128]{1,0:T(4,128)} %bitcast.15, f32[60,243]{1,0:T(8,128)} %bitcast.14, f32[6,54,60]{2,1,0:T(8,128)} %trace_in.1, f32[6,54,60]{2,1,0:T(8,128)} %bitcast.8, ...), custom_call_target="tpu_custom_call" | custom-call | tf_op jit(solution)/shard_map/pallas_call | solution.py:315
  16.8 0.7 %multiply_add_fusion = (f32[240,128]{1,0:T(8,128)}, f32[240,128]{1,0:T(8,128)}) fusion(f32[240,128]{1,0:T(8,128)S(1)} %get-tuple-element.5, f32[240,128]{1,0:T(8,128)S(1)} %get-tuple-element.6, f32[240,128]{1,0:T(8,128)S(1)} %get-tuple-element.7), kind=kLoop, calls=%fused_computation | loop fusion | flops 122880 | bytes 614400 | tf_op jit(solution)/shard_map/add | solution.py:352
